TPU v7x, 1024 devices: a whole 8x8x8 slice. The times are simulated.
1024 devices in a mesh: atoms: 64 (over y, z), space: 16 (over x, core).
Axes of the slice: x: 8, y: 8, z: 8, core: 2. Of those that a mesh axis runs over, the one named last changes fastest.
Arguments:
- block_store: bfloat16 [16, 256, 128, 128], P('space', 'atoms'), may hold values from -0.21875 to 0.21875
- block_source: int32 [64, 16, 36], P('atoms', 'space'), may hold values from 0 to 255, as said below
- chem_pot: float32 [1], replicated, may hold values from -0.6 to 0.6
- basis_values: bfloat16 [64, 16, 8, 128, 1024], P('atoms', 'space'), may hold values from -1.5 to 1.5
- core_density: float32 [64, 16, 1024], P('atoms', 'space'), may hold values from 0.5 to 4
- point_weights: float32 [64, 16, 1024], P('atoms', 'space'), may hold values from 0.2 to 0.8
- pair_dest: int32 [64, 16, 12], P('atoms', 'space'), may hold values from 0 to 15, as said below
- tile_pairs: int32 [64, 16, 2, 16], P('atoms', 'space'), may hold values from -1 to 7, as said below
Outputs:
- density: bfloat16 [64, 16, 768, 128], P('atoms', 'space')
- potential: float32 [64, 16, 1024], P('atoms', 'space')
- kohn_sham: float32 [64, 16, 768, 128], P('atoms', 'space')
Inputs may be any that keep to these rules, and one draw needn't show every extreme that they name: `block_source`: each device names at most 1 block whose number // 4 is the same; blocks may repeat. `pair_dest`: the two pairs of one density block go to different tiles; a device sends at most 1 pairs to one tile. `tile_pairs`: slots that receive no pair hold -1 in both entries; the others follow the pairs as stated.
All inputs are finite; a program needn't handle non-finite values.
Results may differ from a plain program's by a relative error of at most 0.0065.
Values may be sent and summed in bfloat16 or wider, within the bound.
A program may use at most 32 MiB of HBM per device.

v0:
```python
import math

import jax
import jax.numpy as jnp
from jax import lax
from jax.sharding import PartitionSpec as P

KB = 6


slater_factor = math.pow(3.0 / math.pi, 1.0 / 3.0)
density_floor = 0.05


def earlier_count(labels):
    order = jnp.arange(labels.shape[0])
    earlier = (labels[None, :] == labels[:, None]) & (order[None, :] < order[:, None])
    return jnp.sum(earlier.astype(jnp.int32), axis=1)


def sign_density(blocks, chem):
    block_width = blocks.shape[-1]
    order_full = KB * block_width
    matrix = (
        blocks.reshape(KB, KB, block_width, block_width)
        .transpose(0, 2, 1, 3)
        .reshape(order_full, order_full)
    )
    widened = matrix.astype(jnp.float32)
    identity = jnp.eye(order_full, dtype=jnp.float32)
    shifted = 0.5 * (widened + widened.T) - chem * identity
    scaling = 2.0 * jnp.sqrt(jnp.sum(shifted * shifted) / order_full + 1e-06)
    start_x = (shifted / scaling).astype(jnp.bfloat16)
    square_one = jnp.dot(start_x, start_x, preferred_element_type=jnp.float32)
    factor_one = (1.5 * identity - 0.5 * square_one).astype(jnp.bfloat16)
    next_x = jnp.dot(start_x, factor_one, preferred_element_type=jnp.float32).astype(jnp.bfloat16)
    square_two = jnp.dot(next_x, next_x[:, :block_width], preferred_element_type=jnp.float32)
    factor_two = (1.5 * identity[:, :block_width] - 0.5 * square_two).astype(jnp.bfloat16)
    final_x = jnp.dot(next_x, factor_two, preferred_element_type=jnp.float32)
    return (0.5 * (identity[:, :block_width] - final_x)).astype(jnp.bfloat16)


def per_device(
    block_store,
    block_source,
    chem_pot,
    basis_values,
    core_density,
    point_weights,
    pair_dest,
    tile_pairs,
):
    stored = block_store[0]
    block_width = stored.shape[-1]
    source = block_source[0, 0]
    slot_count = source.shape[0]
    space_devices = lax.axis_size("space")
    initial = jnp.zeros((slot_count, block_width, block_width), jnp.bfloat16)
    shard_rows = lax.all_gather(block_store, "atoms", axis=1, tiled=True)
    count_here = shard_rows.shape[1]
    inside = (source >= 0) & (source < count_here)
    taken = jnp.take(shard_rows[0], jnp.clip(source, 0, count_here - 1), axis=0)
    blocks = jnp.where(inside[:, None, None], taken, initial)
    density = sign_density(blocks, chem_pot[0])
    destinations = pair_dest[0, 0]
    send_count = destinations.shape[0]
    tile_capacity = (send_count + space_devices - 1) // space_devices
    slot_total = space_devices * tile_capacity
    send_slot = destinations * tile_capacity + earlier_count(destinations)
    placed = (send_slot[None, :] == jnp.arange(slot_total)[:, None]).astype(jnp.bfloat16)
    owner_block = (jnp.arange(send_count)[:, None] // 2 == jnp.arange(KB)[None, :]).astype(
        jnp.bfloat16
    )
    routing = jnp.dot(placed, owner_block, preferred_element_type=jnp.float32).astype(jnp.bfloat16)
    column_blocks = density.reshape(KB, block_width, block_width)
    outgoing = jnp.einsum(
        "rk,kab->rab", routing, column_blocks, preferred_element_type=jnp.float32
    ).astype(jnp.bfloat16)
    incoming = lax.all_to_all(
        outgoing.reshape(space_devices, tile_capacity, block_width, block_width),
        "space",
        split_axis=0,
        concat_axis=0,
        tiled=True,
    )
    incoming = incoming.reshape(slot_total, block_width, block_width)
    row_pick = tile_pairs[0, 0, 0]
    col_pick = tile_pairs[0, 0, 1]
    tables = basis_values[0, 0]
    table_count = tables.shape[0]
    points = tables.shape[-1]

    def accumulate(total, items):
        pair_block, row_at, col_at = items
        left_basis = jnp.take(tables, jnp.clip(row_at, 0, table_count - 1), axis=0)
        right_basis = jnp.take(tables, jnp.clip(col_at, 0, table_count - 1), axis=0)
        product = jnp.dot(pair_block, right_basis, preferred_element_type=jnp.float32)
        term = jnp.sum(left_basis.astype(jnp.float32) * product, axis=0)
        return (total + (row_at >= 0).astype(jnp.float32) * term, None)

    valence, _ = lax.scan(
        accumulate, jnp.zeros((points,), jnp.float32), (incoming, row_pick, col_pick)
    )
    potential = -slater_factor * jnp.cbrt(jnp.maximum(core_density[0, 0] + valence, density_floor))
    scaled = point_weights[0, 0] * potential

    def project(unused, items):
        row_at, col_at = items
        left_basis = jnp.take(tables, jnp.clip(row_at, 0, table_count - 1), axis=0)
        right_basis = jnp.take(tables, jnp.clip(col_at, 0, table_count - 1), axis=0)
        weighted = (left_basis.astype(jnp.float32) * scaled[None, :]).astype(jnp.bfloat16)
        partial_value = lax.dot_general(
            weighted, right_basis, (((1,), (1,)), ((), ())), preferred_element_type=jnp.float32
        )
        return (unused, partial_value.astype(jnp.bfloat16))

    _, partials = lax.scan(project, jnp.zeros((), jnp.float32), (row_pick, col_pick))
    returned = lax.all_to_all(
        partials.reshape(space_devices, tile_capacity, block_width, block_width),
        "space",
        split_axis=0,
        concat_axis=0,
        tiled=True,
    )
    returned = returned.reshape(slot_total, block_width, block_width)
    kohn = jnp.einsum("rk,rab->kab", routing, returned, preferred_element_type=jnp.float32)
    kohn = kohn.reshape(KB * block_width, block_width)
    return (density[None, None], potential[None, None], kohn[None, None])


def solution(mesh):
    placed = (
        P("space", "atoms", None, None),
        P("atoms", "space", None),
        P(),
        P("atoms", "space", None, None, None),
        P("atoms", "space", None),
        P("atoms", "space", None),
        P("atoms", "space", None),
        P("atoms", "space", None, None),
    )
    return jax.shard_map(
        per_device,
        mesh=mesh,
        in_specs=placed,
        out_specs=(
            P("atoms", "space", None, None),
            P("atoms", "space", None),
            P("atoms", "space", None, None),
        ),
        check_vma=False,
    )
```

profile of v0, /device:TPU:1, one launch (start us, length us, event | category | flops | bytes accessed | tf_op | source)
XLA Modules:
  0.0 348.8 jit_solution(11022087729265415980)
XLA Ops:
  13.6 117.5 %all-gather.2.cloned.1.call-done = bf16[1,256,128,128]{3,2,0,1:T(8,128)(2,1)} async-done(((bf16[1,4,128,128]{3,2,0,1:T(8,128)(2,1)}), bf16[1,256,128,128]{3,2,0,1:T(8,128)(2,1)}) %all-gather.2.cloned.1.call-update) | async-done | bytes 8388624 | tf_op jit(solution)/shard_map/all_gather | solution.py:59
  131.0 5.3 %gather_fusion = bf16[36,128,128]{2,1,0:T(8,128)(2,1)} fusion(bf16[256,128,128]{2,1,0:T(8,128)(2,1)} %bitcast.115, s32[1024]{0:T(1024)S(1)} %pad_clamp_fusion), kind=kCustom, calls=%fused_computation | custom fusion | bytes 2359440 | tf_op jit(solution)/shard_map/jit(_take)/gather | solution.py:62
  136.3 2.1 fusion.27
  138.5 2.0 copy.53
  140.4 3.0 copy.33
  143.5 3.0 multiply_reduce_fusion
  147.2 7.2 %convolution_convert_fusion.1 = bf16[768,768]{1,0:T(8,128)(2,1)S(1)} fusion(f32[]{:T(128)S(6)} %mul_shard_map.3, f32[768,768]{1,0:T(8,128)} %bitcast.108, f32[768,768]{0,1:T(8,128)} %copy.33, f32[]{:T(128)} %bitcast.104), kind=kOutput, calls=%fused_computation.40 | convolution fusion | flops 1823735808 | bytes 5898248 | tf_op jit(solution)/shard_map/dot_general | solution.py:36
  154.4 2.3 fusion.31
  158.0 7.5 %all-to-all-start = ((bf16[16,1,128,128]{3,2,1,0:T(8,128)(2,1)}), bf16[16,1,128,128]{3,2,1,0:T(8,128)(2,1)S(1)}, u32[]{:S(2)}, u32[]{:S(2)}) async-start(bf16[16,1,128,128]{3,2,1,0:T(8,128)(2,1)} %copy.35), calls=%async_computation | async-start | bytes 1048576 | tf_op jit(solution)/shard_map/all_to_all | solution.py:79
  165.5 17.3 %all-to-all-done = bf16[16,1,128,128]{3,2,1,0:T(8,128)(2,1)S(1)} async-done(((bf16[16,1,128,128]{3,2,1,0:T(8,128)(2,1)}), bf16[16,1,128,128]{3,2,1,0:T(8,128)(2,1)S(1)}, u32[]{:S(2)}, u32[]{:S(2)}) %all-to-all-start) | async-done | bytes 524320 | tf_op jit(solution)/shard_map/all_to_all | solution.py:79
  182.8 72.4 %while.23 = (s32[]{:T(128)}, f32[1024]{0:T(1024)S(1)}, s32[16]{0:T(128)S(1)}, bf16[8,128,1024]{2,1,0:T(8,128)(2,1)}, bf16[16,128,128]{2,1,0:T(8,128)(2,1)S(1)}, ...) while((s32[]{:T(128)}, f32[1024]{0:T(1024)S(1)}, ...), condition=%wide.region_4.6_spmd.clone, body=%wide.region_2.5_spmd.clone.sunk | while | flops 34211856 | bytes 574289 | solution.py:101
  189.9 1.3 fusion.73
  203.4 1.3 fusion.73
  217.0 1.3 fusion.73
  255.9 64.8 %while.22 = (s32[]{:T(128)}, bf16[16,128,128]{2,1,0:T(8,128)(2,1)S(1)}, s32[16]{0:T(128)S(1)}, bf16[8,128,1024]{2,1,0:T(8,128)(2,1)}, f32[1024]{0:T(1024)S(1)}, ...) while((s32[]{:T(128)}, ...), condition=%wide.region_6.8_spmd, body=%wide.region_5.7_spmd.sunk | while | flops 34226192 | bytes 561973 | solution.py:117
  258.6 1.3 fusion.70
  262.6 1.3 fusion.70
  266.7 1.3 fusion.70
  270.7 1.3 fusion.70
  274.8 1.3 fusion.70
  278.8 1.3 fusion.70
  282.9 1.3 fusion.70
  287.0 1.3 fusion.70
  291.0 1.3 fusion.70
  295.1 1.3 fusion.70
  299.1 1.3 fusion.70
  303.2 1.3 fusion.70
  307.2 1.3 fusion.70
  311.3 1.3 fusion.70
  315.3 1.3 fusion.70
  319.4 1.3 fusion.70
  320.7 20.1 %all_to_all.10 = bf16[16,1,128,128]{3,2,1,0:T(8,128)(2,1)S(1)} all-to-all(bf16[16,1,128,128]{3,2,1,0:T(8,128)(2,1)S(1)} %bitcast.110), channel_id=1, replica_groups=mesh['atoms'=64,'space'=16] {'space'}, dimensions={0} | all-to-all | bytes 1048576 | tf_op jit(solution)/shard_map/all_to_all | solution.py:118
  (122 shorter events, 66.7 us)
Async XLA Ops:
  7.2 123.9 %all-gather.2.cloned.1.call-start = ((), (), s32[]{:S(2)}) async-start(), calls=%async_computation.2 | async-start | bytes 8519680 | tf_op jit(solution)/shard_map/all_gather | solution.py:59
  156.6 26.2 %copy-start = (bf16[768,128]{1,0:T(8,128)(2,1)}, bf16[768,128]{1,0:T(8,128)(2,1)S(1)}, u32[]{:S(2)}) copy-start(bf16[768,128]{1,0:T(8,128)(2,1)S(1)} %fusion.31) | copy-start | bytes 589828
  156.7 8.9 %copy-start.3 = (s32[1,1,2,16]{3,2,1,0:T(2,128)S(1)}, s32[1,1,2,16]{3,2,1,0:T(2,128)}, u32[]{:S(2)}) copy-start(s32[1,1,2,16]{3,2,1,0:T(2,128)} %param.21) | copy-start | bytes 388
  158.0 24.9 %all-to-all-start = ((bf16[16,1,128,128]{3,2,1,0:T(8,128)(2,1)}), bf16[16,1,128,128]{3,2,1,0:T(8,128)(2,1)S(1)}, u32[]{:S(2)}, u32[]{:S(2)}) async-start(bf16[16,1,128,128]{3,2,1,0:T(8,128)(2,1)} %copy.35), calls=%async_computation | async-start | bytes 1048576 | tf_op jit(solution)/shard_map/all_to_all | solution.py:79
  182.8 72.4 %copy-start.1 = (f32[1,1,1024]{2,1,0:T(1,128)S(1)}, f32[1,1,1024]{2,1,0:T(1,128)}, u32[]{:S(2)}) copy-start(f32[1,1,1024]{2,1,0:T(1,128)} %param.19) | copy-start | bytes 12292
  182.8 72.4 %copy-start.2 = (f32[1,1,1024]{2,1,0:T(1,128)S(1)}, f32[1,1,1024]{2,1,0:T(1,128)}, u32[]{:S(2)}) copy-start(f32[1,1,1024]{2,1,0:T(1,128)} %param.18) | copy-start | bytes 12292
Sparse Core Ops, SparseCore 0:
  12.2 118.8 all-gather.1
where the time goes:
time: 351 us; the launch traced here: 349 us
  waiting for transfers between devices  135 us (38%)
  loops' own time  55 us (16%)
  local copies, waits for them, and re-layouts  53.5 us (15%)
  matrix products  51.3 us (15%)
  blocking collectives  20.1 us (6%)
  between operations  15.5 us (4%)
  other arithmetic  10.5 us (3%)
  starting transfers between devices  7.57 us (2%)
    all_gather x1, waiting for transfers between devices, per_device(): shard_rows = lax.all_gather(block_store, 'atoms', axis=1, tiled=True)  117 us
    dynamic_slice x64, local copies, waits for them, and re-layouts, per_device(): lax.scan(accumulate, jnp.zeros((points,), jnp.float32), (incoming, row_pi...  41.3 us
    another operation x1, loops' own time, per_device(): lax.scan(accumulate, jnp.zeros((points,), jnp.float32), (incoming, row_pi...  32.1 us
    another operation x1, loops' own time, per_device(): lax.scan(project, jnp.zeros((), jnp.float32), (row_pick, col_pick))  22.9 us
    dot_general x16, matrix products, project(): lax.dot_general(weighted, right_basis, (((1,), (1,)), ((), ())), preferre...  20.6 us
    dot_general x16, matrix products, accumulate(): jnp.dot(pair_block, right_basis, preferred_element_type=jnp.float32)  20.2 us
    all_to_all x1, blocking collectives, per_device(): lax.all_to_all(partials.reshape(space_devices, tile_capacity, block_width...  20.1 us
    all_to_all x1, waiting for transfers between devices, per_device(): lax.all_to_all(outgoing.reshape(space_devices, tile_capacity, block_width...  17.3 us
  transfers between devices with their start and end apart: 2, of which 2 were waited for; matrix products, arithmetic and copies ran while one was open for 1% of the time, Pallas kernels for 0%

commit v1 on v0

v1 whole, which is shorter than its diff:
```python
import math

import jax
import jax.numpy as jnp
from jax import lax
from jax.experimental import pallas as pl
from jax.experimental.pallas import tpu as pltpu
from jax.sharding import PartitionSpec as P

RING = 8
CORES = 2
SPACE = RING * CORES
B = 128
H = B // 2
KB = 6
M = KB * B
SLOTS = KB * KB
SENDS = 2 * KB
NB = 4
NLOC = 8
PTS = 1024
SLATER = math.pow(3.0 / math.pi, 1.0 / 3.0)
FLOOR = 0.05
MESH = pl.DeviceIdType.MESH
GROUPS = ((0, 1), (1, 2), (3, 2), (5, 2), (7, 1))


def ring_offset(r):
    half = (r + 1) // 2
    return half - 2 * half * (r % 2)


def ring_rank(d):
    return jnp.where(d < RING // 2, 2 * d, 2 * (RING - d) - 1)


def kernel(
    store_ref,
    source_ref,
    chem_ref,
    basis_hbm,
    core_ref,
    weight_ref,
    dest_ref,
    pairs_ref,
    density_hbm,
    potential_ref,
    kohn_hbm,
    *scratch,
):
    held = (scratch[0:8], scratch[8:16])
    (
        want_out,
        want_in,
        want_sm,
        out0,
        out1,
        in0,
        in1,
        shifted,
        x_mat,
        t_mat,
        x1_mat,
        tables,
        density,
        pair_out,
        pair_in,
        part_out,
        part_in,
        kohn,
        local_sem,
        want_send,
        want_recv,
        ring_send,
        ring_recv,
        slot_send,
        slot_recv,
        pair_send,
        pair_recv,
        part_send,
        part_recv,
    ) = scratch[16:]
    outs, ins = (out0, out1), (in0, in1)
    atom, space = lax.axis_index("atoms"), lax.axis_index("space")
    y, z = atom // RING, atom % RING
    x, core = space // CORES, space % CORES
    me = (y, z)

    def across(h, at):
        return (at * RING + z, space) if h == 0 else (y * RING + at, space)

    def along(h, off):
        if h == 0:
            return (y * RING + (z + off) % RING, space)
        return (((y + off) % RING) * RING + z, space)

    barrier = pltpu.get_barrier_semaphore()
    for off in range(1, RING):
        for h in range(2):
            pl.semaphore_signal(barrier, inc=1, device_id=along(h, off), device_id_type=MESH)
    for off in range(1, SPACE):
        other = (atom, (space + off) % SPACE)
        pl.semaphore_signal(barrier, inc=1, device_id=other, device_id_type=MESH)

    basis_copy = pltpu.make_async_copy(basis_hbm, tables, local_sem.at[0])
    basis_copy.start()
    for h in range(2):
        held[h][0][...] = store_ref[:, h * H : (h + 1) * H, :]

    row = lax.broadcasted_iota(jnp.int32, (RING, B), 0)
    off = ring_offset(lax.broadcasted_iota(jnp.int32, (RING, B), 1))
    peer0 = row * RING + (z + off + RING * B) % RING
    peer1 = ((y + off + RING * B) % RING) * RING + row
    want0 = jnp.zeros((RING, B), jnp.int32)
    want1 = jnp.zeros((RING, B), jnp.int32)
    for m in range(SLOTS):
        number = source_ref[m]
        want0 = jnp.where(peer0 == number // NB, number % NB, want0)
        want1 = jnp.where(peer1 == number // NB, number % NB, want1)
    for h, want in enumerate((want0, want1)):
        want_out[h] = want
        want_in[h, me[h]] = want

    pl.semaphore_wait(barrier, 2 * (RING - 1) + SPACE - 1)

    def ring_copies(step):
        copies = []
        for h in range(2):
            for way in range(2):
                if step < 4:
                    src = held[h][0 if step == 1 else 2 * step - 3 + way]
                    dst = held[h][2 * step - 1 + way]
                else:
                    src = held[h][5 + way].at[pl.ds(2 * way, 2)]
                    dst = held[h][7].at[pl.ds(2 * way, 2)]
                copies.append(
                    pltpu.make_async_remote_copy(
                        src_ref=src,
                        dst_ref=dst,
                        send_sem=ring_send.at[h, way, step - 1],
                        recv_sem=ring_recv.at[h, way, step - 1],
                        device_id=along(h, 1 if way == 0 else RING - 1),
                        device_id_type=MESH,
                    )
                )
        return copies

    rings = [ring_copies(step) for step in range(1, 5)]
    for copy in rings[0]:
        copy.start()
    wants = []
    for h in range(2):
        for n in range(RING - 1, 0, -1):
            at = (me[h] + ring_offset(n) + RING) % RING
            wants.append(
                pltpu.make_async_remote_copy(
                    src_ref=want_out.at[h],
                    dst_ref=want_in.at[h, me[h]],
                    send_sem=want_send.at[h, n - 1],
                    recv_sem=want_recv.at[h, n - 1],
                    device_id=across(h, at),
                    device_id_type=MESH,
                )
            )
            wants[-1].start()
    for copy in wants:
        copy.wait()
    to_scalar = pltpu.make_async_copy(want_in, want_sm, local_sem.at[1])
    to_scalar.start()
    to_scalar.wait()

    def pick(h, at, first, count):
        for r in range(first, first + count):
            outs[h][at, r] = held[h][r][want_sm[h, at, me[h], r]]

    for group, (first, count) in enumerate(GROUPS):
        if group > 0:
            for copy in rings[group - 1]:
                copy.wait_recv()
        if 0 < group < 4:
            for copy in rings[group]:
                copy.start()

        def send_slots(i, carry, first=first, count=count):
            for h in range(2):
                at = (me[h] + ring_offset(RING - 1 - i) + RING) % RING
                pick(h, at, first, count)
                pltpu.make_async_remote_copy(
                    src_ref=outs[h].at[at, pl.ds(first, count)],
                    dst_ref=ins[h].at[me[h], pl.ds(first, count)],
                    send_sem=slot_send.at[h],
                    recv_sem=slot_recv.at[h],
                    device_id=across(h, at),
                    device_id_type=MESH,
                ).start()
            return carry

        lax.fori_loop(0, RING - 1, send_slots, 0)
        for h in range(2):
            for r in range(first, first + count):
                ins[h][me[h], r] = held[h][r][want_sm[h, me[h], me[h], r]]

    owner = []
    for n in range(SPACE):
        tile = ((x + ring_offset(n // CORES) + RING) % RING) * CORES + (core + n % CORES) % CORES
        block = 0
        for j in range(SENDS):
            block = jnp.where(dest_ref[j] == tile, j // 2, block)
        owner.append((tile, block))

    for h in range(2):
        most = ins[h].at[pl.ds(0, RING - 1)]
        pltpu.make_async_copy(most, most, slot_recv.at[h]).wait()

    eye = (
        lax.broadcasted_iota(jnp.int32, (B, B), 0) == lax.broadcasted_iota(jnp.int32, (B, B), 1)
    ).astype(jnp.float32)
    chem = chem_ref[0]

    def block(i, j):
        peer = source_ref[i * KB + j] // NB
        py, pz = peer // RING, peer % RING
        top = in0[py, ring_rank((pz - z + RING) % RING)]
        low = in1[pz, ring_rank((py - y + RING) % RING)]
        return jnp.concatenate([top, low], axis=0)

    upper = [(i, j) for i in range(KB) for j in range(i, KB)]
    total = jnp.zeros((8, B), jnp.float32)
    for n, (i, j) in enumerate(upper):
        here = block(i, j)
        there = here if i == j else block(j, i)
        value = 0.5 * (here.astype(jnp.float32) + there.T.astype(jnp.float32))
        if i == j:
            value = value - chem * eye
        shifted[n] = value
        square = jnp.sum((value * value).reshape(B // 8, 8, B), axis=0)
        total = total + (square if i == j else 2.0 * square)
    scale = 2.0 * jnp.sqrt(jnp.sum(total, keepdims=True) / M + 1e-06)
    factor = 1.0 / scale
    for n, (i, j) in enumerate(upper):
        value = (shifted[n] * factor).astype(jnp.bfloat16)
        x_mat[i * B : (i + 1) * B, j * B : (j + 1) * B] = value
        if i != j:
            x_mat[j * B : (j + 1) * B, i * B : (i + 1) * B] = value.T

    wide = 2 * B

    def identity(n):
        rows = lax.broadcasted_iota(jnp.int32, (M, wide), 0)
        columns = lax.broadcasted_iota(jnp.int32, (M, wide), 1) + n * wide
        return (rows == columns).astype(jnp.float32)

    for n in range(M // wide):
        at = slice(n * wide, (n + 1) * wide)
        square = jnp.dot(x_mat[...], x_mat[:, at], preferred_element_type=jnp.float32)
        t_mat[:, at] = (1.5 * identity(n) - 0.5 * square).astype(jnp.bfloat16)
    for n in range(M // wide):
        at = slice(n * wide, (n + 1) * wide)
        x1_mat[:, at] = jnp.dot(
            x_mat[...], t_mat[:, at], preferred_element_type=jnp.float32
        ).astype(jnp.bfloat16)
    first_columns = identity(0)[:, :B]
    square = jnp.dot(x1_mat[...], x1_mat[:, :B], preferred_element_type=jnp.float32)
    t2 = (1.5 * first_columns - 0.5 * square).astype(jnp.bfloat16)
    final = jnp.dot(x1_mat[...], t2, preferred_element_type=jnp.float32)
    density[...] = (0.5 * (first_columns - final)).astype(jnp.bfloat16).reshape(KB, B, B)
    density_copy = pltpu.make_async_copy(density, density_hbm, local_sem.at[2])
    density_copy.start()

    def mirror(n):
        rank, other = n // CORES, n % CORES
        if rank not in (0, RING - 1):
            rank = rank + 1 if rank % 2 else rank - 1
        return rank * CORES + other

    pair_in[0] = density[owner[0][1]]
    pair_copies = []
    for n in range(SPACE - 1, 0, -1):
        tile, number = owner[n]
        pair_out[n] = density[number]
        pair_copies.append(
            pltpu.make_async_remote_copy(
                src_ref=pair_out.at[n],
                dst_ref=pair_in.at[mirror(n)],
                send_sem=pair_send.at[n],
                recv_sem=pair_recv.at[mirror(n)],
                device_id=(atom, tile),
                device_id_type=MESH,
            )
        )
        pair_copies[-1].start()
    basis_copy.wait()

    def place(n):
        at = (x + ring_offset(n // CORES) + RING) % RING
        return at * CORES + (core + n) % CORES

    def values_of(n, row_col):
        return pairs_ref[row_col, place(n)]

    def add_pair(n, valence):
        def arrived():
            pltpu.make_async_copy(pair_in.at[n], pair_in.at[n], pair_recv.at[n]).wait()

        pl.when(n > 0)(arrived)
        left, right = values_of(n, 0), values_of(n, 1)
        product = jnp.dot(
            pair_in[n], tables[jnp.maximum(right, 0)], preferred_element_type=jnp.float32
        )
        term = tables[jnp.maximum(left, 0)].astype(jnp.float32) * product
        term = jnp.sum(term.reshape(B // 8, 8, PTS), axis=0)
        return valence + jnp.where(left >= 0, term, 0.0)

    valence = lax.fori_loop(0, SPACE, add_pair, jnp.zeros((8, PTS), jnp.float32))
    valence = jnp.sum(valence, axis=0, keepdims=True)
    charge = jnp.maximum(core_ref[...] + valence, FLOOR)
    potential = -SLATER * jnp.exp(jnp.log(charge) * (1.0 / 3.0))
    potential_ref[...] = potential
    scaled = weight_ref[...] * potential

    def project(i, carry):
        n = SPACE - 1 - i
        left, right = values_of(n, 0), values_of(n, 1)
        weighted = tables[jnp.maximum(left, 0)].astype(jnp.float32) * scaled
        value = lax.dot_general(
            weighted.astype(jnp.bfloat16),
            tables[jnp.maximum(right, 0)],
            (((1,), (1,)), ((), ())),
            preferred_element_type=jnp.float32,
        ).astype(jnp.bfloat16)
        part_out[n] = value

        def send():
            pltpu.make_async_remote_copy(
                src_ref=part_out.at[n],
                dst_ref=part_in.at[space],
                send_sem=part_send,
                recv_sem=part_recv,
                device_id=(atom, place(n)),
                device_id_type=MESH,
            ).start()

        def keep():
            part_in[space] = value

        pl.when(n > 0)(send)
        pl.when(n == 0)(keep)
        return carry

    lax.fori_loop(0, SPACE, project, 0)
    most = part_in.at[pl.ds(0, SPACE - 1)]
    pltpu.make_async_copy(most, most, part_recv).wait()
    kohn_copies = []
    for k in range(KB):
        one, two = part_in[dest_ref[2 * k]], part_in[dest_ref[2 * k + 1]]
        kohn[k] = one.astype(jnp.float32) + two.astype(jnp.float32)
        kohn_copies.append(pltpu.make_async_copy(kohn.at[k], kohn_hbm.at[k], local_sem.at[3 + k]))
        kohn_copies[-1].start()

    for step in rings:
        for copy in step:
            copy.wait_send()
    for h in range(2):
        most = outs[h].at[pl.ds(0, RING - 1)]
        pltpu.make_async_copy(most, most, slot_send.at[h]).wait()
    for copy in pair_copies:
        copy.wait_send()
    most = part_out.at[pl.ds(1, SPACE - 1)]
    pltpu.make_async_copy(most, most, part_send).wait()
    density_copy.wait()
    for copy in kohn_copies:
        copy.wait()


def per_device(
    block_store,
    block_source,
    chem_pot,
    basis_values,
    core_density,
    point_weights,
    pair_dest,
    tile_pairs,
):
    bf16, f32 = jnp.bfloat16, jnp.float32
    vmem = pl.BlockSpec(memory_space=pltpu.VMEM)
    smem = pl.BlockSpec(memory_space=pltpu.SMEM)
    hbm = pl.BlockSpec(memory_space=pl.ANY)
    dma = pltpu.SemaphoreType.DMA
    density, potential, kohn = pl.pallas_call(
        kernel,
        out_shape=(
            jax.ShapeDtypeStruct((KB, B, B), bf16),
            jax.ShapeDtypeStruct((1, PTS), f32),
            jax.ShapeDtypeStruct((KB, B, B), f32),
        ),
        in_specs=[vmem, smem, smem, hbm, vmem, vmem, smem, smem],
        out_specs=(hbm, vmem, hbm),
        scratch_shapes=[pltpu.VMEM((NB, H, B), bf16)] * 16
        + [
            pltpu.VMEM((2, RING, B), jnp.int32),
            pltpu.VMEM((2, RING, RING, B), jnp.int32),
            pltpu.SMEM((2, RING, RING, B), jnp.int32),
            pltpu.VMEM((RING, RING, H, B), bf16),
            pltpu.VMEM((RING, RING, H, B), bf16),
            pltpu.VMEM((RING, RING, H, B), bf16),
            pltpu.VMEM((RING, RING, H, B), bf16),
            pltpu.VMEM((KB * (KB + 1) // 2, B, B), f32),
            pltpu.VMEM((M, M), bf16),
            pltpu.VMEM((M, M), bf16),
            pltpu.VMEM((M, M), bf16),
            pltpu.VMEM((NLOC, B, PTS), bf16),
            pltpu.VMEM((KB, B, B), bf16),
            pltpu.VMEM((SPACE, B, B), bf16),
            pltpu.VMEM((SPACE, B, B), bf16),
            pltpu.VMEM((SPACE, B, B), bf16),
            pltpu.VMEM((SPACE, B, B), bf16),
            pltpu.VMEM((KB, B, B), f32),
            dma((3 + KB,)),
            dma((2, RING - 1)),
            dma((2, RING - 1)),
            dma((2, 2, 4)),
            dma((2, 2, 4)),
            dma((2,)),
            dma((2,)),
            dma((SPACE,)),
            dma((SPACE,)),
            dma,
            dma,
        ],
        compiler_params=pltpu.CompilerParams(
            collective_id=0, has_side_effects=True, vmem_limit_bytes=48 * 2**20
        ),
        name="grid_exchange",
    )(
        block_store[0],
        block_source[0, 0],
        chem_pot,
        basis_values[0, 0],
        core_density[0],
        point_weights[0],
        pair_dest[0, 0],
        tile_pairs[0, 0],
    )
    return (
        density.reshape(1, 1, M, B),
        potential[None],
        kohn.reshape(1, 1, M, B),
    )


def solution(mesh):
    placed = (
        P("space", "atoms", None, None),
        P("atoms", "space", None),
        P(),
        P("atoms", "space", None, None, None),
        P("atoms", "space", None),
        P("atoms", "space", None),
        P("atoms", "space", None),
        P("atoms", "space", None, None),
    )
    return jax.shard_map(
        per_device,
        mesh=mesh,
        in_specs=placed,
        out_specs=(
            P("atoms", "space", None, None),
            P("atoms", "space", None),
            P("atoms", "space", None, None),
        ),
        check_vma=False,
    )
```

time: 351 us -> 103 us (0.29)
  waiting for transfers between devices: 135 us -> 0 us
  Pallas kernels: 0 us -> 93.4 us
  loops' own time: 55 us -> 0 us
  matrix products: 51.3 us -> 0 us
  local copies, waits for them, and re-layouts: 53.5 us -> 7.87 us
  blocking collectives: 20.1 us -> 0 us
  between operations: 15.5 us -> 1.3 us
  other arithmetic: 10.5 us -> 0 us
  starting transfers between devices: 7.57 us -> 0 us
    all_gather x1 -> x0, waiting for transfers between devices: 117 us -> none  [per_device(): shard_rows = lax.all_gather(block_store, 'atoms', axis=1, tiled=True)]
    pallas_call x0 -> x1, Pallas kernels: none -> 93.4 us  [per_device(): pl.pallas_call(kernel, out_shape=(jax.ShapeDtypeStruct((KB, B, B), bf16),...]
    another operation x2 -> x0, loops' own time: 55 us -> none  [the longest x1 32.1 us: per_device(): lax.scan(accumulate, jnp.zeros((points,), jnp.float32), (incoming, row_pi...]
    dot_general x37 -> x0, matrix products: 51.3 us -> none  [the longest x16 20.6 us: project(): lax.dot_general(weighted, right_basis, (((1,), (1,)), ((), ())), preferre...]
    dynamic_slice x64 -> x0, local copies, waits for them, and re-layouts: 41.3 us -> none  [per_device(): lax.scan(accumulate, jnp.zeros((points,), jnp.float32), (incoming, row_pi...]
    all_to_all x1 -> x0, blocking collectives: 20.1 us -> none  [per_device(): lax.all_to_all(partials.reshape(space_devices, tile_capacity, block_width...]
    all_to_all x1 -> x0, waiting for transfers between devices: 17.3 us -> none  [per_device(): lax.all_to_all(outgoing.reshape(space_devices, tile_capacity, block_width...]
    all_to_all x1 -> x0, starting transfers between devices: 7.54 us -> none  [per_device(): lax.all_to_all(outgoing.reshape(space_devices, tile_capacity, block_width...]
  transfers between devices with their start and end apart: 2 -> 0, of which waited for: 2 -> 0; matrix products, arithmetic and copies ran while one was open for 1% -> 0% of each run, Pallas kernels for 0% -> 0%
where the time goes in v1:
time: 103 us
  Pallas kernels  93.4 us (91%)
  local copies, waits for them, and re-layouts  7.87 us (8%)
  between operations  1.3 us (1%)
    pallas_call x1, Pallas kernels, per_device(): pl.pallas_call(kernel, out_shape=(jax.ShapeDtypeStruct((KB, B, B), bf16),...  93.4 us
    unnamed x17, local copies, waits for them, and re-layouts  7.87 us

profile of v1, /device:TPU:1, one launch (start us, length us, event | category | flops | bytes accessed | tf_op | source)
XLA Modules:
  0.0 102.6 jit_solution(4208149546720677335)
XLA Ops:
  1.3 0.0 copy-start
  1.3 1.6 %copy-done = bf16[1,1,8,128,1024]{4,3,2,1,0:T(8,128)(2,1)S(1)} copy-done((bf16[1,1,8,128,1024]{4,3,2,1,0:T(8,128)(2,1)S(1)}, bf16[1,1,8,128,1024]{4,3,2,1,0:T(8,128)(2,1)}, u32[]{:S(2)}) %copy-start) | copy-done | bytes 2097176
  2.9 0.0 copy-start.1
  2.9 0.9 copy-done.1
  3.8 0.0 copy-start.2
  3.8 0.7 copy-done.2
  4.5 0.0 copy-start.3
  4.5 0.7 copy-done.3
  5.2 0.0 copy-start.4
  5.2 0.7 copy-done.4
  5.8 0.0 copy-start.5
  5.8 0.7 copy-done.5
  6.5 0.0 copy-start.6
  6.5 0.7 copy-done.6
  7.1 93.4 %grid_exchange.1 = (bf16[6,128,128]{2,1,0:T(8,128)(2,1)S(1)}, f32[1,1024]{1,0:T(1,128)S(1)}, f32[6,128,128]{2,1,0:T(8,128)S(1)}) custom-call(bf16[4,128,128]{2,1,0:T(8,128)(2,1)S(1)} %bitcast.13, s32[36]{0:T(128)S(1)} %bitcast.18, f32[1]{0:T(128)S(6)} %copy.14.chem_ref, bf16[8,128,1024]{2,1,0:T(8,128)(2,1)S(1)} %bitcast.10, f32[1,1024]{1,0:T(1,128)S(1)} %bitcast.14, ...), custom_call_target="tpu_custom_call" | custom-call | tf_op jit(solution)/shard_map/grid_exchange/pallas_call | solution.py:390
  100.6 0.7 copy.15
  101.2 0.6 copy.16
  101.8 0.7 copy.17
Async XLA Ops:
  1.3 1.6 %copy-start = (bf16[1,1,8,128,1024]{4,3,2,1,0:T(8,128)(2,1)S(1)}, bf16[1,1,8,128,1024]{4,3,2,1,0:T(8,128)(2,1)}, u32[]{:S(2)}) copy-start(bf16[1,1,8,128,1024]{4,3,2,1,0:T(8,128)(2,1)} %param.11) | copy-start | bytes 6291460
  2.9 0.9 copy-start.1
  3.8 0.7 copy-start.2
  4.5 0.7 copy-start.3
  5.2 0.7 copy-start.4
  5.8 0.7 copy-start.5
  6.5 0.7 copy-start.6

commit v2 on v1

--- a/solution.py
+++ b/solution.py
@@ -22,7 +22,7 @@
 SLATER = math.pow(3.0 / math.pi, 1.0 / 3.0)
 FLOOR = 0.05
 MESH = pl.DeviceIdType.MESH
-GROUPS = ((0, 1), (1, 2), (3, 2), (5, 2), (7, 1))
+GROUPS = ((0, 3), (3, 2), (5, 3))
 
 
 def ring_offset(r):
@@ -35,17 +35,17 @@
 
 
 def kernel(
-    store_ref,
-    source_ref,
+    store_hbm,
+    source_hbm,
     chem_ref,
     basis_hbm,
-    core_ref,
-    weight_ref,
-    dest_ref,
-    pairs_ref,
-    density_hbm,
+    core_hbm,
+    weight_hbm,
+    dest_hbm,
+    pairs_hbm,
+    density,
     potential_ref,
-    kohn_hbm,
+    kohn,
     *scratch,
 ):
     held = (scratch[0:8], scratch[8:16])
@@ -62,12 +62,16 @@
         t_mat,
         x1_mat,
         tables,
-        density,
         pair_out,
         pair_in,
         part_out,
         part_in,
-        kohn,
+        store_ref,
+        source_ref,
+        core_ref,
+        weight_ref,
+        dest_ref,
+        pairs_ref,
         local_sem,
         want_send,
         want_recv,
@@ -94,6 +98,21 @@
             return (y * RING + (z + off) % RING, space)
         return (((y + off) % RING) * RING + z, space)
 
+    copies_in = []
+    for n, (src, dst) in enumerate(
+        (
+            (source_hbm, source_ref),
+            (store_hbm, store_ref),
+            (dest_hbm, dest_ref),
+            (pairs_hbm, pairs_ref),
+            (core_hbm, core_ref),
+            (weight_hbm, weight_ref),
+            (basis_hbm, tables),
+        )
+    ):
+        copies_in.append(pltpu.make_async_copy(src, dst, local_sem.at[n]))
+        copies_in[-1].start()
+
     barrier = pltpu.get_barrier_semaphore()
     for off in range(1, RING):
         for h in range(2):
@@ -102,8 +121,8 @@
         other = (atom, (space + off) % SPACE)
         pl.semaphore_signal(barrier, inc=1, device_id=other, device_id_type=MESH)
 
-    basis_copy = pltpu.make_async_copy(basis_hbm, tables, local_sem.at[0])
-    basis_copy.start()
+    for copy in copies_in[:2]:
+        copy.wait()
     for h in range(2):
         held[h][0][...] = store_ref[:, h * H : (h + 1) * H, :]
 
@@ -146,6 +165,14 @@
         return copies
 
     rings = [ring_copies(step) for step in range(1, 5)]
+
+    def ring_arrived(step):
+        for copy in rings[step - 1]:
+            copy.wait_recv()
+        if step < 4:
+            for copy in rings[step]:
+                copy.start()
+
     for copy in rings[0]:
         copy.start()
     wants = []
@@ -163,9 +190,10 @@
                 )
             )
             wants[-1].start()
+    ring_arrived(1)
     for copy in wants:
         copy.wait()
-    to_scalar = pltpu.make_async_copy(want_in, want_sm, local_sem.at[1])
+    to_scalar = pltpu.make_async_copy(want_in, want_sm, local_sem.at[7])
     to_scalar.start()
     to_scalar.wait()
 
@@ -174,12 +202,8 @@
             outs[h][at, r] = held[h][r][want_sm[h, at, me[h], r]]
 
     for group, (first, count) in enumerate(GROUPS):
-        if group > 0:
-            for copy in rings[group - 1]:
-                copy.wait_recv()
-        if 0 < group < 4:
-            for copy in rings[group]:
-                copy.start()
+        for step in ((2,), (3, 4))[group - 1] if group > 0 else ():
+            ring_arrived(step)
 
         def send_slots(i, carry, first=first, count=count):
             for h in range(2):
@@ -200,6 +224,8 @@
             for r in range(first, first + count):
                 ins[h][me[h], r] = held[h][r][want_sm[h, me[h], me[h], r]]
 
+    for copy in copies_in[2:]:
+        copy.wait()
     owner = []
     for n in range(SPACE):
         tile = ((x + ring_offset(n // CORES) + RING) % RING) * CORES + (core + n % CORES) % CORES
@@ -264,8 +290,6 @@
     t2 = (1.5 * first_columns - 0.5 * square).astype(jnp.bfloat16)
     final = jnp.dot(x1_mat[...], t2, preferred_element_type=jnp.float32)
     density[...] = (0.5 * (first_columns - final)).astype(jnp.bfloat16).reshape(KB, B, B)
-    density_copy = pltpu.make_async_copy(density, density_hbm, local_sem.at[2])
-    density_copy.start()
 
     def mirror(n):
         rank, other = n // CORES, n % CORES
@@ -289,7 +313,6 @@
             )
         )
         pair_copies[-1].start()
-    basis_copy.wait()
 
     def place(n):
         at = (x + ring_offset(n // CORES) + RING) % RING
@@ -350,12 +373,9 @@
     lax.fori_loop(0, SPACE, project, 0)
     most = part_in.at[pl.ds(0, SPACE - 1)]
     pltpu.make_async_copy(most, most, part_recv).wait()
-    kohn_copies = []
     for k in range(KB):
         one, two = part_in[dest_ref[2 * k]], part_in[dest_ref[2 * k + 1]]
         kohn[k] = one.astype(jnp.float32) + two.astype(jnp.float32)
-        kohn_copies.append(pltpu.make_async_copy(kohn.at[k], kohn_hbm.at[k], local_sem.at[3 + k]))
-        kohn_copies[-1].start()
 
     for step in rings:
         for copy in step:
@@ -367,8 +387,17 @@
         copy.wait_send()
     most = part_out.at[pl.ds(1, SPACE - 1)]
     pltpu.make_async_copy(most, most, part_send).wait()
-    density_copy.wait()
-    for copy in kohn_copies:
+
+
+def write_out(density, potential, kohn, density_hbm, potential_hbm, kohn_hbm, sems):
+    copies = [
+        pltpu.make_async_copy(density, density_hbm, sems.at[0]),
+        pltpu.make_async_copy(potential, potential_hbm, sems.at[1]),
+        pltpu.make_async_copy(kohn, kohn_hbm, sems.at[2]),
+    ]
+    for copy in copies:
+        copy.start()
+    for copy in copies:
         copy.wait()
 
 
@@ -385,7 +414,7 @@
     bf16, f32 = jnp.bfloat16, jnp.float32
     vmem = pl.BlockSpec(memory_space=pltpu.VMEM)
     smem = pl.BlockSpec(memory_space=pltpu.SMEM)
-    hbm = pl.BlockSpec(memory_space=pl.ANY)
+    hbm = pl.BlockSpec(memory_space=pltpu.HBM)
     dma = pltpu.SemaphoreType.DMA
     density, potential, kohn = pl.pallas_call(
         kernel,
@@ -394,8 +423,8 @@
             jax.ShapeDtypeStruct((1, PTS), f32),
             jax.ShapeDtypeStruct((KB, B, B), f32),
         ),
-        in_specs=[vmem, smem, smem, hbm, vmem, vmem, smem, smem],
-        out_specs=(hbm, vmem, hbm),
+        in_specs=[hbm, hbm, smem, hbm, hbm, hbm, hbm, hbm],
+        out_specs=(vmem, vmem, vmem),
         scratch_shapes=[pltpu.VMEM((NB, H, B), bf16)] * 16
         + [
             pltpu.VMEM((2, RING, B), jnp.int32),
@@ -410,13 +439,17 @@
             pltpu.VMEM((M, M), bf16),
             pltpu.VMEM((M, M), bf16),
             pltpu.VMEM((NLOC, B, PTS), bf16),
-            pltpu.VMEM((KB, B, B), bf16),
             pltpu.VMEM((SPACE, B, B), bf16),
             pltpu.VMEM((SPACE, B, B), bf16),
             pltpu.VMEM((SPACE, B, B), bf16),
             pltpu.VMEM((SPACE, B, B), bf16),
-            pltpu.VMEM((KB, B, B), f32),
-            dma((3 + KB,)),
+            pltpu.VMEM((NB, B, B), bf16),
+            pltpu.SMEM((SLOTS,), jnp.int32),
+            pltpu.VMEM((1, PTS), f32),
+            pltpu.VMEM((1, PTS), f32),
+            pltpu.SMEM((SENDS,), jnp.int32),
+            pltpu.SMEM((2, SPACE), jnp.int32),
+            dma((8,)),
             dma((2, RING - 1)),
             dma((2, RING - 1)),
             dma((2, 2, 4)),
@@ -429,7 +462,7 @@
             dma,
         ],
         compiler_params=pltpu.CompilerParams(
-            collective_id=0, has_side_effects=True, vmem_limit_bytes=48 * 2**20
+            collective_id=0, has_side_effects=True, vmem_limit_bytes=58000 * 2**10
         ),
         name="grid_exchange",
     )(
@@ -442,6 +475,18 @@
         pair_dest[0, 0],
         tile_pairs[0, 0],
     )
+    density, potential, kohn = pl.pallas_call(
+        write_out,
+        out_shape=(
+            jax.ShapeDtypeStruct((KB, B, B), bf16),
+            jax.ShapeDtypeStruct((1, PTS), f32),
+            jax.ShapeDtypeStruct((KB, B, B), f32),
+        ),
+        in_specs=[vmem] * 3,
+        out_specs=(hbm, hbm, hbm),
+        scratch_shapes=[dma((3,))],
+        name="write_out",
+    )(density, potential, kohn)
     return (
         density.reshape(1, 1, M, B),
         potential[None],

time: 103 us -> 98.5 us (0.956)
  local copies, waits for them, and re-layouts: 7.87 us -> 0 us
  Pallas kernels: 93.4 us -> 97 us
    unnamed x17 -> x0, local copies, waits for them, and re-layouts: 7.87 us -> none
    pallas_call x0 -> x1, Pallas kernels: none -> 1.95 us  [per_device(): pl.pallas_call(write_out, out_shape=(jax.ShapeDtypeStruct((KB, B, B), bf1...]
    pallas_call x1, Pallas kernels: 93.4 us -> 95.1 us  [per_device(): pl.pallas_call(kernel, out_shape=(jax.ShapeDtypeStruct((KB, B, B), bf16),...]
where the time goes in v2:
time: 98.5 us; the launch traced here: 98.3 us
  Pallas kernels  97 us (98%)
  between operations  1.29 us (1%)
    pallas_call x1, Pallas kernels, per_device(): pl.pallas_call(kernel, out_shape=(jax.ShapeDtypeStruct((KB, B, B), bf16),...  95.1 us

profile of v2, /device:TPU:1, one launch (start us, length us, event | category | flops | bytes accessed | tf_op | source)
XLA Modules:
  0.0 98.3 jit_solution(6755372491918832182)
XLA Ops:
  1.3 95.1 %grid_exchange.1 = (bf16[6,128,128]{2,1,0:T(8,128)(2,1)}, f32[1,1024]{1,0:T(1,128)}, f32[6,128,128]{2,1,0:T(8,128)}) custom-call(bf16[4,128,128]{2,1,0:T(8,128)(2,1)} %bitcast.11, s32[36]{0:T(128)} %bitcast.15, f32[1]{0:T(128)S(6)} %copy.11.chem_ref, bf16[8,128,1024]{2,1,0:T(8,128)(2,1)} %bitcast.10, f32[1,1024]{1,0:T(1,128)} %bitcast.12, ...), custom_call_target="tpu_custom_call" | custom-call | tf_op jit(solution)/shard_map/grid_exchange/pallas_call | solution.py:419
  96.4 1.9 %write_out.1 = (bf16[6,128,128]{2,1,0:T(8,128)(2,1)}, f32[1,1024]{1,0:T(1,128)}, f32[6,128,128]{2,1,0:T(8,128)}) custom-call(bf16[6,128,128]{2,1,0:T(8,128)(2,1)} %get-tuple-element.9.density, f32[1,1024]{1,0:T(1,128)} %get-tuple-element.10.potential, f32[6,128,128]{2,1,0:T(8,128)} %get-tuple-element.11.kohn), custom_call_target="tpu_custom_call" | custom-call | tf_op jit(solution)/shard_map/write_out/pallas_call | solution.py:478

commit v3 on v2

--- a/solution.py
+++ b/solution.py
@@ -341,19 +341,22 @@
     potential_ref[...] = potential
     scaled = weight_ref[...] * potential
 
-    def project(i, carry):
-        n = SPACE - 1 - i
+    def partial(n):
         left, right = values_of(n, 0), values_of(n, 1)
         weighted = tables[jnp.maximum(left, 0)].astype(jnp.float32) * scaled
-        value = lax.dot_general(
+        return lax.dot_general(
             weighted.astype(jnp.bfloat16),
             tables[jnp.maximum(right, 0)],
             (((1,), (1,)), ((), ())),
             preferred_element_type=jnp.float32,
         ).astype(jnp.bfloat16)
-        part_out[n] = value
-
-        def send():
+
+    def project(i, carry):
+        places = [SPACE - 1 - 3 * i - k for k in range(3)]
+        values = [partial(n) for n in places]
+        for n, value in zip(places, values):
+            part_out[n] = value
+        for n in places:
             pltpu.make_async_remote_copy(
                 src_ref=part_out.at[n],
                 dst_ref=part_in.at[space],
@@ -362,15 +365,10 @@
                 device_id=(atom, place(n)),
                 device_id_type=MESH,
             ).start()
-
-        def keep():
-            part_in[space] = value
-
-        pl.when(n > 0)(send)
-        pl.when(n == 0)(keep)
         return carry
 
-    lax.fori_loop(0, SPACE, project, 0)
+    lax.fori_loop(0, (SPACE - 1) // 3, project, 0)
+    part_in[space] = partial(0)
     most = part_in.at[pl.ds(0, SPACE - 1)]
     pltpu.make_async_copy(most, most, part_recv).wait()
     for k in range(KB):

time: 98.5 us -> 98.7 us (level)
  no operation moved by 1% of the time
where the time goes in v3:
time: 98.7 us; the launch traced here: 98.5 us
  Pallas kernels  97.2 us (98%)
  between operations  1.29 us (1%)
    pallas_call x1, Pallas kernels, per_device(): pl.pallas_call(kernel, out_shape=(jax.ShapeDtypeStruct((KB, B, B), bf16),...  95.3 us

profile of v3, /device:TPU:1, one launch (start us, length us, event | category | flops | bytes accessed | tf_op | source)
XLA Modules:
  0.0 98.5 jit_solution(13476842059901802473)
XLA Ops:
  1.3 95.3 %grid_exchange.1 = (bf16[6,128,128]{2,1,0:T(8,128)(2,1)}, f32[1,1024]{1,0:T(1,128)}, f32[6,128,128]{2,1,0:T(8,128)}) custom-call(bf16[4,128,128]{2,1,0:T(8,128)(2,1)} %bitcast.11, s32[36]{0:T(128)} %bitcast.15, f32[1]{0:T(128)S(6)} %copy.11.chem_ref, bf16[8,128,1024]{2,1,0:T(8,128)(2,1)} %bitcast.10, f32[1,1024]{1,0:T(1,128)} %bitcast.12, ...), custom_call_target="tpu_custom_call" | custom-call | tf_op jit(solution)/shard_map/grid_exchange/pallas_call | solution.py:417
  96.5 1.9 %write_out.1 = (bf16[6,128,128]{2,1,0:T(8,128)(2,1)}, f32[1,1024]{1,0:T(1,128)}, f32[6,128,128]{2,1,0:T(8,128)}) custom-call(bf16[6,128,128]{2,1,0:T(8,128)(2,1)} %get-tuple-element.9.density, f32[1,1024]{1,0:T(1,128)} %get-tuple-element.10.potential, f32[6,128,128]{2,1,0:T(8,128)} %get-tuple-element.11.kohn), custom_call_target="tpu_custom_call" | custom-call | tf_op jit(solution)/shard_map/write_out/pallas_call | solution.py:476
